TPU v7x, 32 devices: a whole 2x2x4 slice. The times are simulated.
32 devices in a mesh: fsdp: 8 (over z, x), expert: 4 (over y, core).
Axes of the slice: x: 2, y: 2, z: 4, core: 2. Of those that a mesh axis runs over, the one named last changes fastest.
Arguments:
- inputs: bfloat16 [2, 32, 197, 512], P(None, ('fsdp', 'expert')), may hold values from -6 to 6
- gain_attn: bfloat16 [512], P('fsdp'), may hold values from 0.5 to 1.5
- qkv_weight: bfloat16 [512, 1536], P('fsdp'), may hold values from -0.25 to 0.25
- out_weight: bfloat16 [512, 512], P('fsdp'), may hold values from -2 to 2
- gain_moe: bfloat16 [512], P('fsdp'), may hold values from 0.5 to 1.5
- router_weight: bfloat16 [512, 8], P('fsdp'), may hold values from -0.1875 to 0.1875
- expert_in: bfloat16 [8, 512, 2048], P('expert', 'fsdp'), may hold values from -0.25 to 0.25
- expert_out: bfloat16 [8, 2048, 512], P('expert', 'fsdp'), may hold values from -2 to 2
- routes: int32 [2, 32, 197, 2], P(None, ('fsdp', 'expert')), may hold values from 0 to 7, all different within a row; in each aligned block of 197 rows (0 to 196, 197 to 393, ..., all dimensions but the last counted through in order) at most 62 rows name the same one
- cotangent: bfloat16 [2, 32, 197, 512], P(None, ('fsdp', 'expert')), may hold values from -6 to 6
Outputs:
- activations: bfloat16 [2, 32, 197, 512], P(None, ('fsdp', 'expert'))
- input_grad: float32 [2, 32, 197, 512], P(None, ('fsdp', 'expert'))
- grad_gain_attn: float32 [512], P('fsdp')
- grad_qkv: float32 [512, 1536], P('fsdp')
- grad_out: float32 [512, 512], P('fsdp')
- grad_gain_moe: float32 [512], P('fsdp')
- grad_router: float32 [512, 8], P('fsdp')
- grad_expert_in: float32 [8, 512, 2048], P('expert', 'fsdp')
- grad_expert_out: float32 [8, 2048, 512], P('expert', 'fsdp')
Inputs may be any that keep to these rules, and one draw needn't show every extreme that they name: `routes`: each token names two different experts; among the 197 tokens of one device in one micro-batch no expert is named more than 62 times, a bound that some block reaches.
All inputs are finite; a program needn't handle non-finite values.
Results may differ from a plain program's by a relative error of at most 0.023.
Values may be sent and summed in bfloat16 or wider, within the bound.
A program may use at most 128 MiB of HBM per device.

v0:
```python
import functools
import math

import jax
import jax.numpy as jnp
from jax import lax
from jax.experimental import pallas as pl
from jax.experimental.pallas import tpu as pltpu
from jax.sharding import PartitionSpec as P

HEADS = 8
EPS = 1e-06
MESH = pl.DeviceIdType.MESH
F32 = jnp.float32
BF16 = jnp.bfloat16


def nn(a, b):
    return lax.dot_general(a, b, (((1,), (0,)), ((), ())), preferred_element_type=F32)


def nt(a, b):
    return lax.dot_general(a, b, (((1,), (1,)), ((), ())), preferred_element_type=F32)


def tn(a, b):
    return lax.dot_general(a, b, (((0,), (0,)), ((), ())), preferred_element_type=F32)


def normalize(values):
    center = jnp.mean(values, axis=-1, keepdims=True)
    shifted = values - center
    spread = jnp.mean(shifted * shifted, axis=-1, keepdims=True)
    rstd = lax.rsqrt(spread + EPS)
    return shifted * rstd, rstd


def normalize_back(grad, hat, rstd):
    return rstd * (
        grad
        - jnp.mean(grad, axis=-1, keepdims=True)
        - hat * jnp.mean(grad * hat, axis=-1, keepdims=True)
    )


class Semaphores:
    def __init__(self):
        self.used = 0

    def take(self, count):
        start = self.used
        self.used += count
        return start


SIZES = ("nz", "E", "G", "NE", "NR", "T", "TP", "CP", "S", "D", "FC", "RF", "CF", "M")


def layout(mesh_shape, micro, seq, width, ff_width):
    fsdp, peers = mesh_shape["fsdp"], mesh_shape["expert"]
    c = {}
    c["nz"] = fsdp // 2
    c["E"] = peers
    c["G"] = peers // 2
    c["NE"] = 2 * peers
    c["T"] = seq
    c["TP"] = -(-seq // 16) * 16
    c["CP"] = -(-max(2, 10 * seq // (4 * 2 * peers) + 1) // 16) * 16
    c["S"] = c["NE"] * c["CP"]
    c["NR"] = -(-(c["NE"] + 2) // 16) * 16
    c["D"] = width
    c["FF"] = ff_width
    c["RF"] = width // fsdp
    c["CF"] = ff_width // fsdp
    c["FC"] = 2 * c["CF"]
    c["WQ"] = 128 * -(-(3 * width // 128) // peers)
    c["WO"] = 128 * -(-(width // 128) // peers)
    c["M"] = micro
    return c


def scratch_of(c):
    nz, E, G, NE, NR, T, TP, CP, S, D, FC, RF, CF, M = (c[k] for k in SIZES)
    h = nz // 2
    v = {
        "XP": ((M, TP, D), BF16),
        "CT": ((M, TP, D), BF16),
        "XR": ((T, M, D), BF16),
        "CR": ((T, M, D), BF16),
        "AR": ((T, M, D), F32),
        "AO": ((T, M, D), BF16),
        "IG": ((M, T, 1, D), F32),
        "RR": ((M, 2, T), jnp.int32),
        "RT": ((M, TP, 128), F32),
        "SR": ((nz, 2, NR, RF), BF16),
        "G1": ((1, RF), BF16),
        "G2": ((1, RF), BF16),
        "RW": ((NE, RF), BF16),
        "GI": ((2, RF, nz * FC), BF16),
        "GT": ((2, CF, D), BF16),
        "GS": ((NR, RF), F32),
        "SM": ((nz, 2, RF, 128), BF16),
        "WIN": ((nz, nz, 2, RF, FC), BF16),
        "WOUT": ((nz, 2, CF, D), BF16),
        "N1": ((M, TP, D), BF16),
        "J": ((M, TP, 3 * D), BF16),
        "ATT": ((M, TP, D), BF16),
        "MID": ((M, TP, D), F32),
        "N2": ((M, TP, D), BF16),
        "GATES": ((M, TP, 128), F32),
        "PM": ((M, 2, TP, S), BF16),
        "XS": ((M, NE, CP, D), BF16),
        "XB": ((M, NE, CP, D), BF16),
        "GSS": ((M, NE, CP, D), BF16),
        "GRB": ((M, NE, CP, D), BF16),
        "CSS": ((M, NE, 8, 128), F32),
        "CSB": ((M, NE, 8, 128), F32),
        "CROW": ((8, S), F32),
        "GC": ((M, S, D), BF16),
        "YS": ((M, NE, CP, D), BF16),
        "YB": ((M, NE, CP, D), BF16),
        "DXS": ((M, NE, CP, D), BF16),
        "DXB": ((M, NE, CP, D), BF16),
        "GCS": ((M, NE, 8, 128), F32),
        "GCB": ((M, NE, 8, 128), F32),
        "YACC": ((M, S, D), F32),
        "DXACC": ((M, S, D), F32),
        "AS": ((M, S, FC), BF16),
        "GHS": ((M, S, FC), BF16),
        "DWI": ((nz, nz, 2, RF, FC), BF16),
        "DWO": ((nz, 2, CF, D), BF16),
        "UPI": ((nz, nz, 2, RF, FC), BF16),
        "UPO": ((nz, 2, CF, D), BF16),
        "DNI": ((nz, nz, 2, RF, FC), BF16),
        "DNO": ((nz, 2, CF, D), BF16),
        "FXI": ((nz, RF, FC), BF16),
        "FXO": ((CF, D), BF16),
        "GM": ((M, TP, D), F32),
        "GA": ((M, TP, D), BF16),
        "GJ": ((M, TP, 3 * D), BF16),
        "GR": ((NR, D), F32),
        "GB": ((NR, D), BF16),
        "SB1": ((NR, D), BF16),
        "SB2": ((G, NR, D), BF16),
        "SB3": ((2, NR, D), BF16),
        "SB4": ((nz, NR, D), BF16),
    }
    for name, wide in (("Q", c["WQ"]), ("O", c["WO"])):
        for part, lead in (
            ("W", (E, nz, 2)),
            ("G", (E, nz, 2)),
            ("B1", (G, nz, 2)),
            ("Y1", (G, h, 2)),
            ("X1", (G, nz - h)),
            ("X2", (h,)),
            ("Y2", (G, nz - h)),
            ("Z", (nz,)),
            ("F", (E,)),
        ):
            v[name + part] = (lead + (RF, wide), BF16)
    return v


def kernel(c, names, counts, *refs):
    nz, E, G, NE, NR, T, TP, CP, S, D, FC, RF, CF, M = (c[k] for k in SIZES)
    (xin, cot, routes, qkv_s, out_s, gain1, gain2, router, ein, eout) = refs[:10]
    (act, igrad, gqkv, gout, ggain1, ggain2, grouter, gein, geout) = refs[10:19]
    b = dict(zip(names, refs[19:]))
    SS, RS, LS = refs[-3:]
    h = nz // 2
    head = D // HEADS
    pair = 2 * head
    scale = 1.0 / math.sqrt(head)
    sems, sends, locals_ = Semaphores(), Semaphores(), Semaphores()
    pending = []

    f = lax.axis_index("fsdp")
    e = lax.axis_index("expert")
    z, x = f // 2, f % 2
    y, core = e // 2, e % 2
    pme = 2 * e + x

    def at(zz, xx, ee):
        return (zz * 2 + xx, ee)

    sibling = at(z, x, y * 2 + (1 - core))
    across = at(z, 1 - x, e)

    def copy_of(src, dst, ssem, rsem, device):
        return pltpu.make_async_remote_copy(
            src_ref=src,
            dst_ref=dst,
            send_sem=SS.at[ssem],
            recv_sem=RS.at[rsem],
            device_id=device,
            device_id_type=MESH,
        )

    def when(cond, run):
        if cond is None:
            run()
        else:
            pl.when(cond)(run)

    def send(src, dst, ssem, rsem, device, cond=None):
        when(cond, copy_of(src, dst, ssem, rsem, device).start)

    def arrived(dst, rsem, cond=None):
        when(cond, copy_of(dst, dst, 0, rsem, sibling).wait_recv)

    def sent_later(ssem, src, cond=None):
        pending.append((cond, copy_of(src, src, ssem, 0, sibling)))

    def one_send(src, dst, device):
        ssem, rsem = sends.take(1), sems.take(1)
        send(src, dst, ssem, rsem, device)
        sent_later(ssem, src)
        return rsem

    barrier = pltpu.get_barrier_semaphore()
    for dz in range(1, nz):
        pl.semaphore_signal(
            barrier, inc=1, device_id=at((z + dz) % nz, x, e), device_id_type=MESH
        )

    def greet(d, carry):
        p = (pme + d) % NE
        pl.semaphore_signal(barrier, inc=1, device_id=at(z, p % 2, p // 2), device_id_type=MESH)
        return carry

    lax.fori_loop(1, NE, greet, 0)

    SM, WIN, WOUT = b["SM"], b["WIN"], b["WOUT"]
    UP, DN = (b["UPI"], b["UPO"]), (b["DNI"], b["DNO"])

    def fetch(src, dst):
        copy = pltpu.make_async_copy(src, dst, LS.at[locals_.take(1)])
        copy.start()
        return copy

    far_first = [d for k in range(1, nz) for d in (k, nz - k) if 2 * k <= nz]
    orders = list(dict.fromkeys(far_first))

    class Dense:
        def __init__(self, name, shard, wide):
            self.name, self.shard, self.wide = name, shard, wide
            self.w, self.g = b[name + "W"], b[name + "G"]
            self.used = -(-shard.shape[1] // wide)
            self.own = locals_.take(1)
            for k in range(self.used):

                @pl.when(e == k)
                def _():
                    pltpu.make_async_copy(
                        self.columns(shard, k), self.w.at[k, z, x], LS.at[self.own]
                    ).start()

        def columns(self, ref, k):
            return ref.at[:, k * self.wide : (k + 1) * self.wide]

        def own_ready(self):
            copy = pltpu.make_async_copy(
                self.w.at[e, z, x], self.w.at[e, z, x], LS.at[self.own]
            )
            when(None if self.used == E else e < self.used, copy.wait)

        def along_z(self):
            w = self.w
            self.r_z, s_z = sems.take(nz - 1) - 1, sends.take(1)
            for dz in orders:
                to = at((z + dz) % nz, x, e)
                send(w.at[e, z, x], w.at[e, z, x], s_z, self.r_z + dz, to)
            sent_later(s_z, w.at[e, 0 : nz - 1, x])
            self.s_x, self.r_x = sends.take(1), sems.take(nz)
            self.s_y, self.r_y = sends.take(G - 1) - 1, sems.take(G - 1) - 1
            self.s_c, self.r_c = sends.take(1), sems.take(1)
            sent_later(self.s_x, w.at[e, :, x])
            for d in range(1, G):
                sent_later(self.s_y + d, w.at[e, :, x])
            sent_later(self.s_c, w.at[0:G])

        def spread(self, dz):
            zz = (z + nz - dz) % nz
            piece = self.w.at[e, zz, x]
            if dz > 0:
                arrived(piece, self.r_z + dz)
            send(piece, piece, self.s_x, self.r_x + dz, across)
            for d in range(1, G):
                to = at(z, x, ((y + d) % G) * 2 + core)
                send(piece, piece, self.s_y + d, self.r_y + d, to)
            send(piece, piece, self.s_c, self.r_c, sibling)

        def forward(self):
            w = self.w
            self.s_xy, self.r_xy = sends.take(G - 1) - 1, sems.take(G - 1) - 1
            for d in range(1, G):
                sent_later(self.s_xy + d, w.at[e, :, x])
            for dz in [0] + orders:
                piece = w.at[e, (z + nz - dz) % nz, 1 - x]
                arrived(piece, self.r_x + dz)
                for d in range(1, G):
                    to = at(z, x, ((y + d) % G) * 2 + core)
                    send(piece, piece, self.s_xy + d, self.r_xy + d, to)
                send(piece, piece, self.s_c, self.r_c, sibling)

        def corner(self):
            w = self.w
            for d in range(1, G):
                ee = ((y + G - d) % G) * 2 + core
                arrived(w.at[ee, :, x], self.r_y + d)
                send(w.at[ee, :, x], w.at[ee, :, x], self.s_c, self.r_c, sibling)
                arrived(w.at[ee, :, 1 - x], self.r_xy + d)
                send(w.at[ee, :, 1 - x], w.at[ee, :, 1 - x], self.s_c, self.r_c, sibling)

        def ready(self):
            arrived(self.w.at[0:G], self.r_c)

        def blocks(self):
            for k in range(self.used):
                cols = slice(k * self.wide, min((k + 1) * self.wide, self.shard.shape[1]))
                yield cols, self.w[k].reshape(D, self.wide)

        def put(self, left, right):
            for k in range(self.used):
                cols = slice(k * self.wide, (k + 1) * self.wide)
                part = tn(left, right[:, :, cols].reshape(M * TP, self.wide))
                self.g[k] = part.astype(BF16).reshape(nz, 2, RF, self.wide)

        def sum_core(self):
            s, self.r_1 = sends.take(1), sems.take(1)
            for j in range(G):
                send(self.g.at[2 * j + 1 - core], b[self.name + "B1"].at[j], s, self.r_1, sibling)
            sent_later(s, b[self.name + "B1"])

        def sum_plane(self):
            g, first = self.g, b[self.name + "B1"]
            arrived(first, self.r_1)
            for j in range(G):
                g[2 * j + core] = g[2 * j + core] + first[j]
            s, self.r_y1 = sends.take(G - 1) - 1, sems.take(G - 1) - 1
            for d in range(1, G):
                q = (y + d) % G
                piece = g.at[2 * q + core, 0:h]
                send(piece, b[self.name + "Y1"].at[y], s + d, self.r_y1 + d, at(z, x, 2 * q + core))
                sent_later(s + d, piece)
            s, self.r_x1 = sends.take(1), sems.take(1)
            for j in range(G):
                piece = g.at[2 * j + core, h:nz, 1 - x]
                send(piece, b[self.name + "X1"].at[j], s, self.r_x1, across)
            sent_later(s, b[self.name + "X1"])

        def sum_cross(self):
            g, from_y, from_x = self.g, b[self.name + "Y1"], b[self.name + "X1"]
            for d in range(1, G):
                q = (y + G - d) % G
                arrived(from_y.at[q], self.r_y1 + d)
                g[e, 0:h] = g[e, 0:h] + from_y[q]
            self.r_x2 = one_send(g.at[e, 0:h, 1 - x], b[self.name + "X2"], across)
            arrived(from_x, self.r_x1)
            for j in range(G):
                g[2 * j + core, h:nz, x] = g[2 * j + core, h:nz, x] + from_x[j]
            s, self.r_y2 = sends.take(G - 1) - 1, sems.take(G - 1) - 1
            for d in range(1, G):
                q = (y + d) % G
                piece = g.at[2 * q + core, h:nz, x]
                send(piece, b[self.name + "Y2"].at[y], s + d, self.r_y2 + d, at(z, x, 2 * q + core))
                sent_later(s + d, piece)

        def sum_z(self):
            g, from_x, from_y = self.g, b[self.name + "X2"], b[self.name + "Y2"]
            arrived(from_x, self.r_x2)
            g[e, 0:h, x] = g[e, 0:h, x] + from_x[...]
            for d in range(1, G):
                q = (y + G - d) % G
                arrived(from_y.at[q], self.r_y2 + d)
                g[e, h:nz, x] = g[e, h:nz, x] + from_y[q]
            s, self.r_z2 = sends.take(1), sems.take(1)
            parts = b[self.name + "Z"]
            for dz in orders:
                zz = (z + dz) % nz
                send(g.at[e, zz, x], parts.at[z], s, self.r_z2, at(zz, x, e))
            sent_later(s, parts.at[0 : nz - 1])
            parts[z] = g[e, z, x]

        def hand_out(self):
            parts, done = b[self.name + "Z"], b[self.name + "F"]
            arrived(parts.at[0 : nz - 1], self.r_z2)
            total = parts[0].astype(F32)
            for k in range(1, nz):
                total = total + parts[k].astype(F32)
            done[e] = total.astype(BF16)
            s, self.r_f = sends.take(1), sems.take(1)

            def one(d, carry):
                send(done.at[e], done.at[e], s, self.r_f, at(z, x, (e + d) % E))
                return carry

            lax.fori_loop(1, E, one, 0)
            sent_later(s, done.at[0 : E - 1])

        def leave(self, out):
            done = b[self.name + "F"]
            arrived(done.at[0 : E - 1], self.r_f)
            for k in range(self.used):
                kept.append(fetch(done.at[k], self.columns(out, k)))

    qkv, proj = Dense("Q", qkv_s, c["WQ"]), Dense("O", out_s, c["WO"])
    kept = []

    SR = b["SR"]
    SR[z, x] = jnp.zeros((NR, RF), BF16)
    small_in = [
        fetch(gain1, b["G1"]),
        fetch(gain2, b["G2"]),
        fetch(router, b["RW"]),
    ]
    token_in = [fetch(routes, b["RR"]), fetch(xin, b["XR"]), fetch(cot, b["CR"])]
    own_in = locals_.take(1)
    for k in range(nz):
        pltpu.make_async_copy(
            ein.at[x, :, k * FC : (k + 1) * FC], WIN.at[k, z, x], LS.at[own_in]
        ).start()
    own_out = fetch(eout.at[x], WOUT.at[z, x])

    for copy in small_in:
        copy.wait()
    SR[z, x, 0:NE] = b["RW"][...]
    SR[z, x, NE : NE + 1] = b["G1"][...]
    SR[z, x, NE + 1 : NE + 2] = b["G2"][...]
    entry = lax.broadcasted_iota(jnp.int32, (NR, 128), 0)
    place = lax.broadcasted_iota(jnp.int32, (NR, 128), 1)
    pick = (
        ((entry < NE) & (entry == place))
        | ((entry >= NE) & (entry < NE + 2) & (place == entry - NE + 126))
    ).astype(BF16)
    qkv.own_ready()
    proj.own_ready()
    pl.semaphore_wait(barrier, nz - 1 + NE - 1)

    qkv.along_z()
    r_sz, s_sz = sems.take(1), sends.take(1)
    for dz in orders:
        send(SR.at[z, x], SR.at[z, x], s_sz, r_sz, at((z + dz) % nz, x, e))
    sent_later(s_sz, SR.at[0 : nz - 1, x])
    qkv.spread(0)

    s_xi, r_xi = sends.take(1), sems.take(1)
    for k in range(nz):
        send(ein.at[1 - x, :, k * FC : (k + 1) * FC], WIN.at[k, z, x], s_xi, r_xi, across)
    sent_later(s_xi, WIN.at[:, z, x])


    XP, CT, RT, PM = b["XP"], b["CT"], b["RT"], b["PM"]

    @pl.when(z == 0)
    def _():
        UP[0][:, 0] = jnp.zeros((nz, 2, RF, FC), BF16)
        UP[1][0] = jnp.zeros((2, CF, D), BF16)

    @pl.when(z == nz - 1)
    def _():
        DN[0][:, nz - 1] = jnp.zeros((nz, 2, RF, FC), BF16)
        DN[1][nz - 1] = jnp.zeros((2, CF, D), BF16)

    for copy in token_in:
        copy.wait()
    lane = lax.broadcasted_iota(jnp.int32, (TP, 128), 1)
    lane_f = lane.astype(F32)
    swap = (
        lax.broadcasted_iota(jnp.int32, (2, 128), 0) == lax.broadcasted_iota(jnp.int32, (2, 128), 1)
    ).astype(BF16)
    for m in range(M):
        XP[m] = jnp.zeros((TP, D), BF16)
        CT[m] = jnp.zeros((TP, D), BF16)
        RT[m] = jnp.full((TP, 128), -1.0, F32)
        XP[m, 0:T] = b["XR"][:, m, :]
        CT[m, 0:T] = b["CR"][:, m, :]
        RT[m, 0:T] = tn(b["RR"][m].astype(BF16), swap)

    def onehot(m, j):
        return RT[m][:, j : j + 1] == lane_f

    before = (
        lax.broadcasted_iota(jnp.int32, (TP, TP), 1) < lax.broadcasted_iota(jnp.int32, (TP, TP), 0)
    ).astype(BF16)
    spots = lax.broadcasted_iota(jnp.int32, (TP, S), 1).astype(F32)
    for m in range(M):
        first = onehot(m, 0).astype(F32)
        second = onehot(m, 1).astype(F32)
        rank0 = nn(before, first.astype(BF16))
        rank1 = nn(before, second.astype(BF16)) + jnp.sum(first, axis=0, keepdims=True)
        for j, (hot, rank) in enumerate(((first, rank0), (second, rank1))):
            slot = jnp.sum(hot * rank, axis=-1, keepdims=True)
            route = RT[m][:, j : j + 1]
            spot = jnp.where(route >= 0, route * CP + slot, -1.0)
            PM[m, j] = (spots == spot).astype(BF16)

    def turn_of(i):
        return 0 if i == 0 else i % (nz - 1) + 1

    groups = (range(0, 2), range(2, nz))
    s_zi = [[sends.take(1) for _ in groups] for _ in range(2)]
    s_zo = [sends.take(1) for _ in range(2)]
    r_zi = [[sems.take(nz) for _ in groups] for _ in range(2)]
    r_zo = [sems.take(2 * nz) for _ in range(2)]
    for zz in range(nz):
        for side in range(2):
            count = zz + 1 if side == 0 else nz - zz
            if count < nz:
                for g, turns in enumerate(groups):
                    sent_later(s_zi[side][g], WIN.at[0 : len(turns), 0:count], z == zz)
                sent_later(s_zo[side], WOUT.at[0:count], z == zz)

    def reach(side, d, some=None):
        begun = z - d if side == 0 else z + d
        there = (begun >= 0) if side == 0 else (begun < nz)
        last = (z == nz - 1) if side == 0 else (z == 0)
        if some is not None:
            there = there & some(begun)
        return begun, there, there & jnp.logical_not(last)

    def onward(side):
        return at((z + 1) % nz if side == 0 else (z + nz - 1) % nz, x, e)

    def pass_in(g, d, halves=(0, 1)):
        for side in range(2):
            begun, there, goes = reach(side, d)
            r = r_zi[side][g]
            if d > 0:
                arrived(WIN.at[0 : len(groups[g]), begun], r + d, there)
            if d < nz - 1:

                @pl.when(goes)
                def _():
                    for i in groups[g]:
                        k = turn_of(i) if side == 1 else nz - 1 - turn_of(i)
                        for half in halves:
                            piece = WIN.at[k, begun, x if half == 0 else 1 - x]
                            send(piece, piece, s_zi[side][g], r + d + 1, onward(side))

    def pass_out(d, half, late=None):
        xx = x if half == 0 else 1 - x
        for side in range(2):
            odd = nz - 2 if side == 0 else 1
            some = None
            if late is not None:
                some = (lambda begun: begun == odd) if late else (lambda begun: begun != odd)
            begun, there, goes = reach(side, d, some)
            r = r_zo[side] + 2 * d + half
            piece = WOUT.at[begun, xx]
            if d > 0:
                arrived(piece, r, there)
            if d < nz - 1:
                send(piece, piece, s_zo[side], r + 2, onward(side), goes)

    early, others = 0, 1
    GATES, XS, XB, GC, CROW = (b[k] for k in ("GATES", "XS", "XB", "GC", "CROW"))
    GSS, GRB, CSS, CSB = (b[k] for k in ("GSS", "GRB", "CSS", "CSB"))
    GCS, GCB, YS, YB, DXS, DXB = (b[k] for k in ("GCS", "GCB", "YS", "YB", "DXS", "DXB"))

    def exchange(src, dst, m, sem):
        rows = slice(0, 1 if src.shape[2] == 8 else src.shape[2])

        def one(d, carry):
            p = (pme + d) % NE
            send(src.at[m, p, rows], dst.at[m, pme, rows], *sem, at(z, p % 2, p // 2))
            return carry

        lax.fori_loop(1, NE, one, 0)
        sent_later(sem[0], src.at[m, 0 : NE - 1, rows])
        dst[m, pme] = src[m, pme]

    def exchanged(dst, m, sem):
        rows = slice(0, 1 if dst.shape[2] == 8 else dst.shape[2])
        arrived(dst.at[m, 0 : NE - 1, rows], sem[1])

    def pairs():
        return [(sends.take(1), sems.take(1)) for _ in range(M)]

    s_x, s_cs, s_gr, s_dx, s_gc, s_y = (pairs() for _ in range(6))
    for m in range(M):
        GSS[m] = tn(PM[m, 0] + PM[m, 1], CT[m]).astype(BF16).reshape(NE, CP, D)

    for dz in orders[:2]:
        qkv.spread(dz)
    proj.along_z()
    proj.spread(0)
    pltpu.make_async_copy(WIN.at[:, z, x], WIN.at[:, z, x], LS.at[own_in]).wait()
    pass_in(early, 0, (0,))
    for dz in orders[2:]:
        qkv.spread(dz)
    arrived(SR.at[0 : nz - 1, x], r_sz)
    r_sx = one_send(SR.at[:, x], SR.at[:, x], across)
    own_out.wait()
    pass_out(0, 0)
    arrived(WIN.at[:, z, 1 - x], r_xi)
    pass_in(early, 0, (1,))
    qkv.forward()
    for dz in orders:
        proj.spread(dz)
    proj.forward()
    r_xo = one_send(eout.at[1 - x], WOUT.at[z, x], across)
    for m in range(M):
        exchange(GSS, GRB, m, s_gr[m])
    pass_in(others, 0, (0,))
    arrived(SR.at[:, 1 - x], r_sx)
    for zz in range(nz):
        for xx in range(2):
            SM[zz, xx] = tn(SR[zz, xx], pick).astype(BF16)
    qkv.corner()
    qkv.ready()

    small = SM[...].reshape(D, 128)
    gains = nt(pick, small)
    gain_one, gain_two = gains[NE : NE + 1], gains[NE + 1 : NE + 2]
    key_ok = lax.broadcasted_iota(jnp.int32, (1, TP), 1) < T
    low_half = lax.broadcasted_iota(jnp.int32, (1, pair), 1) < head
    N1, J, ATT, MID, N2 = b["N1"], b["J"], b["ATT"], b["MID"], b["N2"]
    def half_of(value, i):
        keep = low_half if i == 0 else jnp.logical_not(low_half)
        return jnp.where(keep, value, jnp.zeros_like(value))

    def softmax_scores(query, keys):
        scores = jnp.where(key_ok, nt(query, keys) * scale, -1e30)
        raised = jnp.exp(scores - jnp.max(scores, axis=-1, keepdims=True))
        return raised * (1.0 / jnp.sum(raised, axis=-1, keepdims=True))

    def columns(base, hp):
        return pl.ds(pl.multiple_of(base + hp * pair, 128), pair)

    def chosen_of(m, j):
        gates = GATES[m]
        return jnp.sum(jnp.where(onehot(m, j), gates, 0.0), axis=-1, keepdims=True)

    def forward(m):
        tokens = XP[m].astype(F32)
        hat, _ = normalize(tokens)
        N1[m] = (hat * gain_one).astype(BF16)
        for cols, block in qkv.blocks():
            J[m, :, cols] = nn(N1[m], block).astype(BF16)

        def attend(hp, carry):
            query, keys, values = (J[m, :, columns(i * D, hp)] for i in range(3))
            total = jnp.zeros((TP, pair), F32)
            for i in range(2):
                probs = softmax_scores(half_of(query, i), keys).astype(BF16)
                total = total + nn(probs, half_of(values, i))
            ATT[m, :, columns(0, hp)] = total.astype(BF16)
            return carry

        lax.fori_loop(0, D // pair, attend, 0)
        if m == 0:
            pass_in(early, 1)
            pass_in(others, 0, (1,))
            proj.corner()
            proj.ready()
        for cols, block in proj.blocks():
            MID[m, :, cols] = XP[m, :, cols].astype(F32) + nn(ATT[m], block)
        hat, _ = normalize(MID[m])
        N2[m] = (hat * gain_two).astype(BF16)
        logits = jnp.where(lane < NE, nn(N2[m], small), -1e30)
        raised = jnp.exp(logits - jnp.max(logits, axis=-1, keepdims=True))
        GATES[m] = raised / jnp.sum(raised, axis=-1, keepdims=True)
        XS[m] = tn(PM[m, 0] + PM[m, 1], N2[m]).astype(BF16).reshape(NE, CP, D)
        weight = PM[m, 0].astype(F32) * chosen_of(m, 0) + PM[m, 1].astype(F32) * chosen_of(m, 1)
        CROW[0:1] = jnp.sum(weight, axis=0, keepdims=True)
        for k in range(NE):
            CSS[m, k, 0:1, 0:CP] = CROW[0:1, k * CP : (k + 1) * CP]

    diagonal = lax.broadcasted_iota(jnp.int32, (CP, 128), 0) == lax.broadcasted_iota(
        jnp.int32, (CP, 128), 1
    )

    def scale_grads(m):
        for p in range(NE):
            by_lane = CSB[m, p, 0:1]
            weight = jnp.sum(jnp.where(diagonal, by_lane, 0.0), axis=1, keepdims=True)
            GC[m, p * CP : (p + 1) * CP] = (weight * GRB[m, p].astype(F32)).astype(BF16)

    for m in range(M):
        forward(m)
        exchange(XS, XB, m, s_x[m])
        exchange(CSS, CSB, m, s_cs[m])
        if m == 0:
            arrived(WOUT.at[z, 1 - x], r_xo)
            pass_out(0, 1, False)
    pass_in(early, 2)
    pass_out(1, 0)
    for d in range(3, nz):
        pass_in(early, d)
    pass_out(1, 1, False)
    pass_in(others, 1)

    YACC, DXACC, AS, GHS = b["YACC"], b["DXACC"], b["AS"], b["GHS"]
    DWI, DWO = b["DWI"], b["DWO"]
    YACC[...] = jnp.zeros_like(YACC)
    DXACC[...] = jnp.zeros_like(DXACC)
    c0, c1 = math.sqrt(2.0 / math.pi), 0.044715

    OWN = (DWI, DWO)
    s_up = [(sends.take(1), sends.take(1)) for _ in range(2)]
    r_up = [(sems.take(nz * nz), sems.take(2 * nz)) for _ in range(2)]

    def expert_part(k, m, loop=True):
        def half(xx, carry):
            cols = pl.ds(pl.multiple_of(xx * CF, 128), CF)
            w_in = WIN[k, :, :, :, cols].reshape(D, CF)
            w_out = WOUT[k, xx]
            hidden = nn(XB[m].reshape(S, D), w_in)
            grad_acted = nt(GC[m], w_out)
            square = hidden * hidden
            bent = jnp.tanh(c0 * hidden * (1.0 + c1 * square))
            acted = (0.5 * hidden * (1.0 + bent)).astype(BF16)
            slope = 0.5 * (1.0 + bent) + 0.5 * c0 * hidden * (1.0 - bent * bent) * (
                1.0 + 3.0 * c1 * square
            )
            grad_hidden = (grad_acted * slope).astype(BF16)
            AS[m, :, cols] = acted
            GHS[m, :, cols] = grad_hidden
            YACC[m] = YACC[m] + nn(acted, w_out)
            DXACC[m] = DXACC[m] + nt(grad_hidden, w_in)
            return carry

        if loop:
            lax.fori_loop(0, 2, half, 0)
        else:
            half(0, 0)
            half(1, 0)

    def expert_weights(k):
        def half(xx, carry):
            cols = pl.ds(pl.multiple_of(xx * CF, 128), CF)
            grads = GC[...].reshape(M * S, D)
            tokens = XB[...].reshape(M * S, D)
            DWO[k, xx] = tn(AS[:, :, cols].reshape(M * S, CF), grads).astype(BF16)
            DWI[k, :, :, :, cols] = (
                tn(tokens, GHS[:, :, cols].reshape(M * S, CF))
                .astype(BF16)
                .reshape(nz, 2, RF, CF)
            )
            return carry

        lax.fori_loop(0, 2, half, 0)

    def sum_step(side, i, begins, parts):
        far = z if side == 0 else nz - 1 - z
        GOT = UP if side == 0 else DN
        turn = ((i % (nz - 1)) + 1) * jnp.minimum(i, 1)
        k = turn if side == 0 else nz - 1 - turn

        def tokens_side(j, carry):
            goal = nz - 1 - j
            t = goal if side == 0 else nz - 1 - goal
            rsem = r_up[side][0] + k * nz + t

            @pl.when(goal > far)
            def _():
                if not begins:
                    arrived(GOT[0].at[k, t], rsem)
                    DWI[k, t] = DWI[k, t] + GOT[0][k, t]
                send(DWI.at[k, t], GOT[0].at[k, t], s_up[side][0], rsem, onward(side))

            return carry

        def results_side():
            for xx in [xx for part, xx in ((1, 1 - x), (2, x)) if part in parts]:
                rsem = r_up[side][1] + 2 * k + xx
                if not begins:
                    arrived(GOT[1].at[k, xx], rsem)
                    DWO[k, xx] = DWO[k, xx] + GOT[1][k, xx]
                send(DWO.at[k, xx], GOT[1].at[k, xx], s_up[side][1], rsem, onward(side))

        if parts != (0,):
            pl.when(turn == nz - 1)(results_side)
        if 0 in parts:
            lax.fori_loop(0, nz - 1, tokens_side, 0)
        if parts != (0,):
            pl.when((turn > far) & (turn < nz - 1))(results_side)

    def sums_begin(i, parts=(0, 1, 2)):
        for side in range(2):
            far = z if side == 0 else nz - 1 - z
            step = functools.partial(sum_step, side, jnp.int32(i), True, parts)
            pl.when(far == 0)(step)

    def sums_pass(far_at, i, parts=(0, 1, 2)):
        for side in range(2):
            far = z if side == 0 else nz - 1 - z
            step = functools.partial(sum_step, side, jnp.int32(i), False, parts)
            pl.when(far == far_at)(step)

    passes = [(far, i, part) for far in range(1, nz - 1) for i in range(nz) for part in range(3)]

    def sums_now(*wanted):
        for step in wanted:
            if step in passes:
                passes.remove(step)
                sums_pass(step[0], step[1], (step[2],))

    def sums_rest():
        for far in range(1, nz - 1):
            left = [step for step in passes if step[0] == far]
            if nz <= 4:
                for _, i, part in left:
                    sums_pass(far, i, (part,))
            else:

                def one(i, carry, far=far):
                    sums_pass(far, i)
                    return carry

                lax.fori_loop(left[0][1], nz, one, 0)

    for zz in range(nz):
        for side in range(2):
            count = nz - 1 - zz if side == 0 else zz
            if count > 0:
                sent_later(s_up[side][0], DWI.at[:, 0:count], z == zz)
                sent_later(s_up[side][1], DWO.at[0:count], z == zz)

    def give_back(m):
        DXS[m] = DXACC[m].astype(BF16).reshape(NE, CP, D)
        exchange(DXS, DXB, m, s_dx[m])
        results = YACC[m].astype(BF16)
        YS[m] = results.reshape(NE, CP, D)
        for p in range(NE):
            rows = slice(p * CP, (p + 1) * CP)
            weight = jnp.sum(
                results[rows].astype(F32) * GRB[m, p].astype(F32), axis=1, keepdims=True
            )
            GCS[m, p, 0:1] = jnp.sum(jnp.where(diagonal, weight, 0.0), axis=0, keepdims=True)
        exchange(GCS, GCB, m, s_gc[m])

    when_two, when_far, when_late = (1, 2, nz - 1) if nz <= 4 else (0, 0, 0)
    for i in range(nz):
        if i == when_two:
            pass_out(2, 0)
            pass_out(2, 1, False)
        if i == when_far:
            pass_in(others, 2)
            pass_out(0, 1, True)
            for d in range(3, nz):
                pass_in(others, d)
                pass_out(d, 0)
                pass_out(d, 1, False)
        if i == when_late:
            for d in range(1, nz):
                pass_out(d, 1, True)
            sums_now((1, 0, 0), (1, 0, 1), (1, 0, 2))
        block = turn_of(i) + (z // h) * (nz - 1 - 2 * turn_of(i))
        for m in range(M):
            if i == 0:
                exchanged(GRB, m, s_gr[m])
                exchanged(XB, m, s_x[m])
                exchanged(CSB, m, s_cs[m])
                scale_grads(m)
            expert_part(block, m, i == 1)
            if i == nz - 1:
                give_back(m)
        if i == nz - 1:
            for m in range(M):
                exchange(YS, YB, m, s_y[m])
        expert_weights(block)
        sums_begin(i)

    r_fin, s_fin = (sems.take(nz), sems.take(1)), (sends.take(1), sends.take(1))
    FX = (b["FXI"], b["FXO"])
    GI, GT = b["GI"], b["GT"]
    sent_later(s_fin[0], FX[0])
    sent_later(s_fin[1], FX[1])

    def total_of(kind, place):
        return (
            OWN[kind][place].astype(F32)
            + UP[kind][place].astype(F32)
            + DN[kind][place].astype(F32)
        )

    def sums_end_in(k):
        cols = pl.ds(pl.multiple_of(k * FC, 128), FC)
        for side, ref, ok in ((0, UP, z > 0), (1, DN, z < nz - 1)):
            arrived(ref[0].at[k, z], r_up[side][0] + k * nz + z, ok)
        FX[0][k] = total_of(0, (k, z, 1 - x)).astype(BF16)
        send(FX[0].at[k], GI.at[x, :, cols], s_fin[0], r_fin[0] + k, across)
        GI[x, :, cols] = total_of(0, (k, z, x)).astype(BF16)

    def sums_end_out(mine):
        xx = x if mine else 1 - x
        for side, ref, ok in ((0, UP, z > 0), (1, DN, z < nz - 1)):
            arrived(ref[1].at[z, xx], r_up[side][1] + 2 * z + xx, ok)
        if mine:
            GT[x] = total_of(1, (z, xx)).astype(BF16)
        else:
            FX[1][...] = total_of(1, (z, xx)).astype(BF16)
            send(FX[1], GT.at[x], s_fin[1], r_fin[1], across)

    at_end = (z == 0) | (z == nz - 1)
    upper = z // h
    first_ends = [nz - 1 - upper * (nz - 1), 1 + upper * (nz - 3)]
    last_ends = [upper * (nz - 1), 2 - upper * (5 - nz)] if nz == 4 else []

    def sums_close():
        kept.append(fetch(GI.at[x], gein.at[x]))
        kept.append(fetch(GT.at[x], geout.at[x]))
        arrived(GT.at[1 - x], r_fin[1])
        kept.append(fetch(GT.at[1 - x], geout.at[1 - x]))
        for k in range(nz):
            arrived(GI.at[1 - x, :, k * FC : (k + 1) * FC], r_fin[0] + k)
        kept.append(fetch(GI.at[1 - x], gein.at[1 - x]))

    GM, GA, GJ, GR = b["GM"], b["GA"], b["GJ"], b["GR"]
    GR[...] = jnp.zeros_like(GR)

    def outputs(m):
        results = YB[m].reshape(S, D)
        out = MID[m] + chosen_of(m, 0) * nn(PM[m, 0], results)
        b["AR"][:, m, :] = (out + chosen_of(m, 1) * nn(PM[m, 1], results))[0:T]

    def backward_top(m):
        upstream = CT[m].astype(F32)
        for k in range(NE):
            CROW[0:1, k * CP : (k + 1) * CP] = GCB[m, k, 0:1, 0:CP]

        def grad_chosen(j):
            return jnp.sum(PM[m, j].astype(F32) * CROW[0:1], axis=-1, keepdims=True)

        gates = GATES[m]
        grad_gates = jnp.where(onehot(m, 0), grad_chosen(0), 0.0) + jnp.where(
            onehot(m, 1), grad_chosen(1), 0.0
        )
        grad_logits = (
            gates * (grad_gates - jnp.sum(grad_gates * gates, axis=-1, keepdims=True))
        ).astype(BF16)
        GR[0:NE] = GR[0:NE] + tn(grad_logits, N2[m])[0:NE]
        grad = nn(PM[m, 0] + PM[m, 1], DXB[m].reshape(S, D)) + nt(grad_logits, small)
        hat, rstd = normalize(MID[m])
        GR[NE + 1 : NE + 2] = GR[NE + 1 : NE + 2] + jnp.sum(grad * hat, axis=0, keepdims=True)
        grad_middle = upstream + normalize_back(grad * gain_two, hat, rstd)
        GM[m] = grad_middle
        branch = grad_middle.astype(BF16)
        N2[m] = branch
        back = None
        for cols, block in proj.blocks():
            term = nt(branch[:, cols], block)
            back = term if back is None else back + term
        GA[m] = back.astype(BF16)

    def backward_heads(m):
        def attend(hp, carry):
            query, keys, values = (J[m, :, columns(i * D, hp)] for i in range(3))
            grads = GA[m, :, columns(0, hp)]
            grad_query = jnp.zeros((TP, pair), F32)
            grad_keys = jnp.zeros((TP, pair), F32)
            grad_values = jnp.zeros((TP, pair), F32)
            for i in range(2):
                part = half_of(query, i)
                upstream = half_of(grads, i)
                probs = softmax_scores(part, keys)
                grad_probs = nt(upstream, values)
                grad_values = grad_values + tn(probs.astype(BF16), upstream)
                grad_scores = (
                    probs
                    * (grad_probs - jnp.sum(grad_probs * probs, axis=-1, keepdims=True))
                ).astype(BF16)
                grad_query = grad_query + nn(grad_scores, half_of(keys, i))
                grad_keys = grad_keys + tn(grad_scores, part)
            GJ[m, :, columns(0, hp)] = (grad_query * scale).astype(BF16)
            GJ[m, :, columns(D, hp)] = (grad_keys * scale).astype(BF16)
            GJ[m, :, columns(2 * D, hp)] = grad_values.astype(BF16)
            return carry

        lax.fori_loop(0, D // pair, attend, 0)

    def backward_end(m, carry):
        grad = None
        for cols, block in qkv.blocks():
            term = nt(GJ[m, :, cols], block)
            grad = term if grad is None else grad + term
        hat, rstd = normalize(XP[m].astype(F32))
        GR[NE : NE + 1] = GR[NE : NE + 1] + jnp.sum(grad * hat, axis=0, keepdims=True)
        full = GM[m] + normalize_back(grad * gain_one, hat, rstd)
        b["IG"][m, :, 0, :] = full[0:T]
        return carry

    sums_now((1, 1, 0), (2, 0, 0))
    for m in range(M):
        exchanged(DXB, m, s_dx[m])
        exchanged(GCB, m, s_gc[m])
        backward_top(m)
        if m == 0:
            sums_now((1, 1, 1))
        if m == M - 1:
            proj.put(ATT[...].reshape(M * TP, D), N2)
            proj.sum_core()
            sums_now((1, 2, 1))
        backward_heads(m)
        if m == 0:
            sums_now((2, 0, 1), (2, 0, 2), (1, 1, 2), (2, 1, 0))
    sums_now((1, 2, 2))
    proj.sum_plane()
    qkv.put(N1[...].reshape(M * TP, D), GJ)
    GB, SB1, SB2, SB3, SB4 = (b[k] for k in ("GB", "SB1", "SB2", "SB3", "SB4"))
    qkv.sum_core()
    lax.fori_loop(0, M, backward_end, 0)
    kept.append(fetch(b["IG"], igrad))
    GB[...] = GR[...].astype(BF16)
    r_b1 = one_send(GB, SB1, sibling)
    qkv.sum_plane()
    proj.sum_cross()
    arrived(SB1, r_b1)
    SB2[y] = GB[...] + SB1[...]
    s_b2, r_b2 = sends.take(G - 1) - 1, sems.take(G - 1) - 1
    for d in range(1, G):
        send(SB2.at[y], SB2.at[y], s_b2 + d, r_b2 + d, at(z, x, ((y + d) % G) * 2 + core))
        sent_later(s_b2 + d, SB2.at[y])
    sums_now((2, 1, 1), (2, 1, 2), (2, 2, 1), (1, 2, 0), (2, 2, 2))
    qkv.sum_cross()
    proj.sum_z()
    if nz == 4:

        @pl.when(at_end)
        def _():
            for k in first_ends:
                sums_end_in(k)

    for d in range(1, G):
        arrived(SB2.at[(y + G - d) % G], r_b2 + d)
    total = SB2[0].astype(F32)
    for j in range(1, G):
        total = total + SB2[j].astype(F32)
    SB3[x] = total.astype(BF16)
    r_b3 = one_send(SB3.at[x], SB3.at[x], across)
    sums_now((1, 3, 0), (1, 3, 1), (1, 3, 2), (2, 2, 0))
    qkv.sum_z()
    arrived(SB3.at[1 - x], r_b3)
    SB4[z] = SB3[0] + SB3[1]
    s_b4, r_b4 = sends.take(1), sems.take(1)
    for dz in orders:
        send(SB4.at[z], SB4.at[z], s_b4, r_b4, at((z + dz) % nz, x, e))
    sent_later(s_b4, SB4.at[0 : nz - 1])
    sums_rest()
    sums_end_out(False)
    if nz == 4:

        @pl.when(jnp.logical_not(at_end))
        def _():
            for k in (0, nz - 1):
                sums_end_in(k)

    proj.hand_out()
    qkv.hand_out()
    if nz == 4:

        @pl.when(at_end)
        def _():
            for k in last_ends:
                sums_end_in(k)

        @pl.when(jnp.logical_not(at_end))
        def _():
            for k in range(1, nz - 1):
                sums_end_in(k)

    else:
        for k in range(nz):
            sums_end_in(k)
    sums_end_out(True)
    for m in range(M):
        exchanged(YB, m, s_y[m])
        outputs(m)
    b["AO"][...] = b["AR"][...].astype(BF16)
    kept.append(fetch(b["AO"], act))
    arrived(SB4.at[0 : nz - 1], r_b4)
    total = SB4[0].astype(F32)
    for k in range(1, nz):
        total = total + SB4[k].astype(F32)
    mine = (
        lax.broadcasted_iota(jnp.int32, (D, RF), 0)
        == lax.broadcasted_iota(jnp.int32, (D, RF), 1) + f * RF
    ).astype(F32)
    b["GS"][...] = lax.dot_general(
        total,
        mine,
        (((1,), (0,)), ((), ())),
        precision=lax.Precision.HIGHEST,
        preferred_element_type=F32,
    )
    kept.append(fetch(b["GS"].at[0:NE], grouter))
    kept.append(fetch(b["GS"].at[NE : NE + 1], ggain1))
    kept.append(fetch(b["GS"].at[NE + 1 : NE + 2], ggain2))
    sums_close()
    proj.leave(gout)
    qkv.leave(gqkv)
    for cond, copy in pending:
        when(cond, copy.wait_send)
    for copy in kept:
        copy.wait()
    used = (sends.used, sems.used, locals_.used)
    assert all(a <= b for a, b in zip(used, counts)), (used, counts)


def hand_over(*refs):
    source, target, held, sem = refs[:9], refs[9:18], refs[18:-1], refs[-1]
    cast = [k for k in range(9) if source[k].dtype != target[k].dtype]
    order = sorted(range(9), key=lambda k: -math.prod(target[k].shape))
    for k in order:
        pltpu.make_async_copy(source[k], held[k], sem.at[0, k]).start()
    for k in order:
        pltpu.make_async_copy(source[k], held[k], sem.at[0, k]).wait()
        ready = held[k]
        if k in cast:
            ready = held[9 + cast.index(k)]
            ready[...] = held[k][...].astype(ready.dtype)
        pltpu.make_async_copy(ready, target[k], sem.at[1, k]).start()
    for k in order:
        pltpu.make_async_copy(target[k], target[k], sem.at[1, k]).wait()


def body(
    mesh_shape,
    inputs,
    gain_attn,
    qkv_weight,
    out_weight,
    gain_moe,
    router_weight,
    expert_in,
    expert_out,
    routes,
    cotangent,
):
    micro, images, seq, width = inputs.shape
    c = layout(mesh_shape, micro, images * seq, width, expert_in.shape[2])
    rows = images * seq
    scratch = scratch_of(c)
    names = list(scratch)
    nz, G = c["nz"], c["G"]
    counts = (48 + 9 * (G - 1), 25 + 19 * nz + 2 * nz * nz + 9 * (G - 1), 19 + 2 * c["E"])
    shapes = (
        ((rows, micro, width), BF16),
        ((micro, rows, 1, width), F32),
        (qkv_weight.shape, F32),
        (out_weight.shape, F32),
        ((1, c["RF"]), F32),
        ((1, c["RF"]), F32),
        ((c["NE"], c["RF"]), F32),
        (expert_in.shape, F32),
        (expert_out.shape, F32),
    )
    shapes = [jax.ShapeDtypeStruct(s, t) for s, t in shapes]
    sums = (2, 3, 7, 8)
    halves = [
        jax.ShapeDtypeStruct(s.shape, BF16 if k in sums else s.dtype) for k, s in enumerate(shapes)
    ]
    anywhere = pl.BlockSpec(memory_space=pltpu.HBM)
    results = pl.pallas_call(
        functools.partial(kernel, c, names, counts),
        out_shape=halves,
        in_specs=[anywhere] * 10,
        out_specs=[anywhere] * 9,
        scratch_shapes=[pltpu.VMEM(s, t) for s, t in scratch.values()]
        + [pltpu.SemaphoreType.DMA((count,)) for count in counts],
        compiler_params=pltpu.CompilerParams(
            collective_id=0, has_side_effects=True, vmem_limit_bytes=60 * 1024 * 1024
        ),
    )(
        jnp.transpose(inputs, (1, 2, 0, 3)).reshape(rows, micro, width),
        jnp.transpose(cotangent, (1, 2, 0, 3)).reshape(rows, micro, width),
        jnp.transpose(routes, (0, 1, 3, 2)).reshape(micro, 2, rows),
        qkv_weight,
        out_weight,
        gain_attn[None, :],
        gain_moe[None, :],
        router_weight.T,
        expert_in,
        expert_out,
    )
    act, igrad, gqkv, gout, ggain1, ggain2, grouter, gein, geout = pl.pallas_call(
        hand_over,
        out_shape=shapes,
        in_specs=[anywhere] * 9,
        out_specs=[anywhere] * 9,
        scratch_shapes=[pltpu.VMEM(s.shape, s.dtype) for s in halves]
        + [pltpu.VMEM(shapes[k].shape, F32) for k in sums]
        + [pltpu.SemaphoreType.DMA((2, 9))],
        compiler_params=pltpu.CompilerParams(vmem_limit_bytes=60 * 1024 * 1024),
    )(*results)
    return (
        jnp.transpose(act.reshape(images, seq, micro, width), (2, 0, 1, 3)),
        igrad.reshape(inputs.shape),
        ggain1[0],
        gqkv,
        gout,
        ggain2[0],
        grouter.T,
        gein,
        geout,
    )


def solution(mesh):
    return jax.shard_map(
        functools.partial(body, dict(mesh.shape)),
        mesh=mesh,
        in_specs=(
            P(None, ("fsdp", "expert"), None, None),
            P("fsdp"),
            P("fsdp", None),
            P("fsdp", None),
            P("fsdp"),
            P("fsdp", None),
            P("expert", "fsdp", None),
            P("expert", "fsdp", None),
            P(None, ("fsdp", "expert"), None, None),
            P(None, ("fsdp", "expert"), None, None),
        ),
        out_specs=(
            P(None, ("fsdp", "expert"), None, None),
            P(None, ("fsdp", "expert"), None, None),
            P("fsdp"),
            P("fsdp", None),
            P("fsdp", None),
            P("fsdp"),
            P("fsdp", None),
            P("expert", "fsdp", None),
            P("expert", "fsdp", None),
        ),
        check_vma=False,
    )
```

profile of v0, /device:TPU:0, one launch (start us, length us, event | category | flops | bytes accessed | tf_op | source)
XLA Modules:
  0.0 137.5 jit_solution(6660323874820355851)
XLA Ops:
  0.6 133.5 %shard_map.169 = (bf16[197,2,512]{2,1,0:T(2,128)(2,1)}, f32[2,197,1,512]{3,2,1,0:T(1,128)}, bf16[64,1536]{1,0:T(8,128)(2,1)}, bf16[64,512]{1,0:T(8,128)(2,1)}, f...) custom-call(bf16[197,2,512]{2,1,0:T(2,128)(2,1)} %bitcast.21, ...), custom_call_target="tpu_custom_call" | custom-call | tf_op jit(solution)/shard_map/pallas_call | solution.py:1156
  134.1 3.2 %shard_map.170 = (bf16[197,2,512]{2,1,0:T(2,128)(2,1)}, f32[2,197,1,512]{3,2,1,0:T(1,128)}, f32[64,1536]{1,0:T(8,128)}, f32[64,512]{1,0:T(8,128)}, f32[1,64]{1,0...) custom-call(bf16[197,2,512]{2,1,0:T(2,128)(2,1)} %get-tuple-element.27.refs_0_, ...), custom_call_target="tpu_custom_call" | custom-call | tf_op jit(solution)/shard_map/pallas_call | solution.py:1178
where the time goes:
time: 138 us; the launch traced here: 137 us
  Pallas kernels  137 us (99%)
    pallas_call x1, Pallas kernels, body(): pl.pallas_call(functools.partial(kernel, c, names, counts), out_shape=hal...  133 us
    pallas_call x1, Pallas kernels, body(): pl.pallas_call(hand_over, out_shape=shapes, in_specs=[anywhere] * 9, out_...  3.15 us

commit v1 on v0

--- a/solution.py
+++ b/solution.py
@@ -108,6 +108,9 @@
         "MID": ((M, TP, D), F32),
         "N2": ((M, TP, D), BF16),
         "GATES": ((M, TP, 128), F32),
+        "PB": ((M, HEADS, TP, TP), BF16),
+        "N1T": ((M, D, TP), BF16),
+        "ATTT": ((M, D, TP), BF16),
         "PM": ((M, 2, TP, S), BF16),
         "XS": ((M, NE, CP, D), BF16),
         "XB": ((M, NE, CP, D), BF16),
@@ -117,9 +120,7 @@
         "CSB": ((M, NE, 8, 128), F32),
         "CROW": ((8, S), F32),
         "GC": ((M, S, D), BF16),
-        "YS": ((M, NE, CP, D), BF16),
         "YB": ((M, NE, CP, D), BF16),
-        "DXS": ((M, NE, CP, D), BF16),
         "DXB": ((M, NE, CP, D), BF16),
         "GCS": ((M, NE, 8, 128), F32),
         "GCB": ((M, NE, 8, 128), F32),
@@ -323,7 +324,9 @@
         def put(self, left, right):
             for k in range(self.used):
                 cols = slice(k * self.wide, (k + 1) * self.wide)
-                part = tn(left, right[:, :, cols].reshape(M * TP, self.wide))
+                part = nn(left[0], right[0, :, cols])
+                for m in range(1, M):
+                    part = part + nn(left[m], right[m, :, cols])
                 self.g[k] = part.astype(BF16).reshape(nz, 2, RF, self.wide)
 
         def sum_core(self):
@@ -556,9 +559,13 @@
     early, others = 0, 1
     GATES, XS, XB, GC, CROW = (b[k] for k in ("GATES", "XS", "XB", "GC", "CROW"))
     GSS, GRB, CSS, CSB = (b[k] for k in ("GSS", "GRB", "CSS", "CSB"))
-    GCS, GCB, YS, YB, DXS, DXB = (b[k] for k in ("GCS", "GCB", "YS", "YB", "DXS", "DXB"))
-
-    def exchange(src, dst, m, sem):
+    GCS, GCB, YB, DXB = (b[k] for k in ("GCS", "GCB", "YB", "DXB"))
+    YS, DXS = XS, GSS
+
+    def gone(src, m, sem):
+        copy_of(src.at[m, 0 : NE - 1], src.at[m, 0 : NE - 1], sem[0], 0, sibling).wait_send()
+
+    def exchange(src, dst, m, sem, later=True):
         rows = slice(0, 1 if src.shape[2] == 8 else src.shape[2])
 
         def one(d, carry):
@@ -567,7 +574,8 @@
             return carry
 
         lax.fori_loop(1, NE, one, 0)
-        sent_later(sem[0], src.at[m, 0 : NE - 1, rows])
+        if later:
+            sent_later(sem[0], src.at[m, 0 : NE - 1, rows])
         dst[m, pme] = src[m, pme]
 
     def exchanged(dst, m, sem):
@@ -601,7 +609,7 @@
     proj.forward()
     r_xo = one_send(eout.at[1 - x], WOUT.at[z, x], across)
     for m in range(M):
-        exchange(GSS, GRB, m, s_gr[m])
+        exchange(GSS, GRB, m, s_gr[m], False)
     pass_in(others, 0, (0,))
     arrived(SR.at[:, 1 - x], r_sx)
     for zz in range(nz):
@@ -643,7 +651,9 @@
             query, keys, values = (J[m, :, columns(i * D, hp)] for i in range(3))
             total = jnp.zeros((TP, pair), F32)
             for i in range(2):
-                probs = softmax_scores(half_of(query, i), keys).astype(BF16)
+                probs = softmax_scores(half_of(query, i), keys)
+                probs = probs.astype(BF16)
+                b["PB"][m, 2 * hp + i] = probs
                 total = total + nn(probs, half_of(values, i))
             ATT[m, :, columns(0, hp)] = total.astype(BF16)
             return carry
@@ -679,7 +689,7 @@
 
     for m in range(M):
         forward(m)
-        exchange(XS, XB, m, s_x[m])
+        exchange(XS, XB, m, s_x[m], False)
         exchange(CSS, CSB, m, s_cs[m])
         if m == 0:
             arrived(WOUT.at[z, 1 - x], r_xo)
@@ -691,6 +701,12 @@
     pass_out(1, 1, False)
     pass_in(others, 1)
 
+    same = (
+        lax.broadcasted_iota(jnp.int32, (D, D), 0) == lax.broadcasted_iota(jnp.int32, (D, D), 1)
+    ).astype(BF16)
+    for m in range(M):
+        b["N1T"][m] = nt(same, N1[m]).astype(BF16)
+        b["ATTT"][m] = nt(same, ATT[m]).astype(BF16)
     YACC, DXACC, AS, GHS = b["YACC"], b["DXACC"], b["AS"], b["GHS"]
     DWI, DWO = b["DWI"], b["DWO"]
     YACC[...] = jnp.zeros_like(YACC)
@@ -763,12 +779,20 @@
             return carry
 
         def results_side():
-            for xx in [xx for part, xx in ((1, 1 - x), (2, x)) if part in parts]:
+            for part, xx, rows in (
+                (1, 1 - x, slice(0, CF)),
+                (2, x, slice(0, CF)),
+                (3, x, slice(0, CF // 2)),
+                (4, x, slice(CF // 2, CF)),
+            ):
+                if part not in parts:
+                    continue
                 rsem = r_up[side][1] + 2 * k + xx
                 if not begins:
                     arrived(GOT[1].at[k, xx], rsem)
                     DWO[k, xx] = DWO[k, xx] + GOT[1][k, xx]
-                send(DWO.at[k, xx], GOT[1].at[k, xx], s_up[side][1], rsem, onward(side))
+                source, target = DWO.at[k, xx, rows], GOT[1].at[k, xx, rows]
+                send(source, target, s_up[side][1], rsem, onward(side))
 
         if parts != (0,):
             pl.when(turn == nz - 1)(results_side)
@@ -819,6 +843,8 @@
                 sent_later(s_up[side][1], DWO.at[0:count], z == zz)
 
     def give_back(m):
+        gone(GSS, m, s_gr[m])
+        gone(XS, m, s_x[m])
         DXS[m] = DXACC[m].astype(BF16).reshape(NE, CP, D)
         exchange(DXS, DXB, m, s_dx[m])
         results = YACC[m].astype(BF16)
@@ -838,7 +864,8 @@
             pass_out(2, 1, False)
         if i == when_far:
             pass_in(others, 2)
-            pass_out(0, 1, True)
+            if nz > 4:
+                pass_out(0, 1, True)
             for d in range(3, nz):
                 pass_in(others, d)
                 pass_out(d, 0)
@@ -861,7 +888,7 @@
             for m in range(M):
                 exchange(YS, YB, m, s_y[m])
         expert_weights(block)
-        sums_begin(i)
+        sums_begin(i, (0, 1, 2) if i < nz - 1 else (0, 1, 3))
 
     r_fin, s_fin = (sems.take(nz), sems.take(1)), (sends.take(1), sends.take(1))
     FX = (b["FXI"], b["FXO"])
@@ -955,9 +982,10 @@
             for i in range(2):
                 part = half_of(query, i)
                 upstream = half_of(grads, i)
-                probs = softmax_scores(part, keys)
+                probs_low = b["PB"][m, 2 * hp + i]
+                probs = probs_low.astype(F32)
                 grad_probs = nt(upstream, values)
-                grad_values = grad_values + tn(probs.astype(BF16), upstream)
+                grad_values = grad_values + tn(probs_low, upstream)
                 grad_scores = (
                     probs
                     * (grad_probs - jnp.sum(grad_probs * probs, axis=-1, keepdims=True))
@@ -982,6 +1010,8 @@
         b["IG"][m, :, 0, :] = full[0:T]
         return carry
 
+    if nz <= 4:
+        pass_out(0, 1, True)
     sums_now((1, 1, 0), (2, 0, 0))
     for m in range(M):
         exchanged(DXB, m, s_dx[m])
@@ -990,7 +1020,7 @@
         if m == 0:
             sums_now((1, 1, 1))
         if m == M - 1:
-            proj.put(ATT[...].reshape(M * TP, D), N2)
+            proj.put(b["ATTT"], N2)
             proj.sum_core()
             sums_now((1, 2, 1))
         backward_heads(m)
@@ -998,7 +1028,7 @@
             sums_now((2, 0, 1), (2, 0, 2), (1, 1, 2), (2, 1, 0))
     sums_now((1, 2, 2))
     proj.sum_plane()
-    qkv.put(N1[...].reshape(M * TP, D), GJ)
+    qkv.put(b["N1T"], GJ)
     GB, SB1, SB2, SB3, SB4 = (b[k] for k in ("GB", "SB1", "SB2", "SB3", "SB4"))
     qkv.sum_core()
     lax.fori_loop(0, M, backward_end, 0)
@@ -1014,8 +1044,6 @@
         send(SB2.at[y], SB2.at[y], s_b2 + d, r_b2 + d, at(z, x, ((y + d) % G) * 2 + core))
         sent_later(s_b2 + d, SB2.at[y])
     sums_now((2, 1, 1), (2, 1, 2), (2, 2, 1), (1, 2, 0), (2, 2, 2))
-    qkv.sum_cross()
-    proj.sum_z()
     if nz == 4:
 
         @pl.when(at_end)
@@ -1030,6 +1058,10 @@
         total = total + SB2[j].astype(F32)
     SB3[x] = total.astype(BF16)
     r_b3 = one_send(SB3.at[x], SB3.at[x], across)
+    qkv.sum_cross()
+    proj.sum_z()
+    if nz == 4:
+        pl.when(at_end)(functools.partial(sums_end_out, False))
     sums_now((1, 3, 0), (1, 3, 1), (1, 3, 2), (2, 2, 0))
     qkv.sum_z()
     arrived(SB3.at[1 - x], r_b3)
@@ -1038,18 +1070,11 @@
     for dz in orders:
         send(SB4.at[z], SB4.at[z], s_b4, r_b4, at((z + dz) % nz, x, e))
     sent_later(s_b4, SB4.at[0 : nz - 1])
+    sums_begin(nz - 1, (4,))
     sums_rest()
-    sums_end_out(False)
-    if nz == 4:
-
-        @pl.when(jnp.logical_not(at_end))
-        def _():
-            for k in (0, nz - 1):
-                sums_end_in(k)
-
-    proj.hand_out()
-    qkv.hand_out()
-    if nz == 4:
+    if nz != 4:
+        sums_end_out(False)
+    else:
 
         @pl.when(at_end)
         def _():
@@ -1058,13 +1083,22 @@
 
         @pl.when(jnp.logical_not(at_end))
         def _():
+            sums_end_out(False)
+            for k in (0, nz - 1):
+                sums_end_in(k)
+
+    proj.hand_out()
+    qkv.hand_out()
+    if nz == 4:
+
+        @pl.when(jnp.logical_not(at_end))
+        def _():
             for k in range(1, nz - 1):
                 sums_end_in(k)
 
     else:
         for k in range(nz):
             sums_end_in(k)
-    sums_end_out(True)
     for m in range(M):
         exchanged(YB, m, s_y[m])
         outputs(m)
@@ -1088,6 +1122,7 @@
     kept.append(fetch(b["GS"].at[0:NE], grouter))
     kept.append(fetch(b["GS"].at[NE : NE + 1], ggain1))
     kept.append(fetch(b["GS"].at[NE + 1 : NE + 2], ggain2))
+    sums_end_out(True)
     sums_close()
     proj.leave(gout)
     qkv.leave(gqkv)

time: 138 us -> 135 us (0.978)
  Pallas kernels: 137 us -> 133 us
    pallas_call x1, Pallas kernels: 133 us -> 130 us  [body(): pl.pallas_call(functools.partial(kernel, c, names, counts), out_shape=hal...]
where the time goes in v1:
time: 135 us; the launch traced here: 134 us
  Pallas kernels  133 us (99%)
    pallas_call x1, Pallas kernels, body(): pl.pallas_call(functools.partial(kernel, c, names, counts), out_shape=hal...  130 us
    pallas_call x1, Pallas kernels, body(): pl.pallas_call(hand_over, out_shape=shapes, in_specs=[anywhere] * 9, out_...  3.15 us

profile of v1, /device:TPU:0, one launch (start us, length us, event | category | flops | bytes accessed | tf_op | source)
XLA Modules:
  0.0 133.8 jit_solution(9007784921702611590)
XLA Ops:
  0.6 129.8 %shard_map.169 = (bf16[197,2,512]{2,1,0:T(2,128)(2,1)}, f32[2,197,1,512]{3,2,1,0:T(1,128)}, bf16[64,1536]{1,0:T(8,128)(2,1)}, bf16[64,512]{1,0:T(8,128)(2,1)}, f...) custom-call(bf16[197,2,512]{2,1,0:T(2,128)(2,1)} %bitcast.21, ...), custom_call_target="tpu_custom_call" | custom-call | tf_op jit(solution)/shard_map/pallas_call | solution.py:1191
  130.4 3.2 %shard_map.170 = (bf16[197,2,512]{2,1,0:T(2,128)(2,1)}, f32[2,197,1,512]{3,2,1,0:T(1,128)}, f32[64,1536]{1,0:T(8,128)}, f32[64,512]{1,0:T(8,128)}, f32[1,64]{1,0...) custom-call(bf16[197,2,512]{2,1,0:T(2,128)(2,1)} %get-tuple-element.27.refs_0_, ...), custom_call_target="tpu_custom_call" | custom-call | tf_op jit(solution)/shard_map/pallas_call | solution.py:1213

commit v2 on v1

--- a/solution.py
+++ b/solution.py
@@ -239,8 +239,9 @@
         copy.start()
         return copy
 
-    far_first = [d for k in range(1, nz) for d in (k, nz - k) if 2 * k <= nz]
-    orders = list(dict.fromkeys(far_first))
+    near_first = [d for k in range(1, nz) for d in (k, nz - k) if 2 * k <= nz]
+    orders = list(dict.fromkeys(near_first))
+    far_first = [j + (1 - z // h) * (nz - 2 * j) for j in range(1, nz)]
 
     class Dense:
         def __init__(self, name, shard, wide):
@@ -379,7 +380,7 @@
                 g[e, h:nz, x] = g[e, h:nz, x] + from_y[q]
             s, self.r_z2 = sends.take(1), sems.take(1)
             parts = b[self.name + "Z"]
-            for dz in orders:
+            for dz in far_first:
                 zz = (z + dz) % nz
                 send(g.at[e, zz, x], parts.at[z], s, self.r_z2, at(zz, x, e))
             sent_later(s, parts.at[0 : nz - 1])
@@ -743,17 +744,15 @@
             half(0, 0)
             half(1, 0)
 
-    def expert_weights(k):
+    def expert_weights(k, first, second):
         def half(xx, carry):
             cols = pl.ds(pl.multiple_of(xx * CF, 128), CF)
-            grads = GC[...].reshape(M * S, D)
-            tokens = XB[...].reshape(M * S, D)
-            DWO[k, xx] = tn(AS[:, :, cols].reshape(M * S, CF), grads).astype(BF16)
-            DWI[k, :, :, :, cols] = (
-                tn(tokens, GHS[:, :, cols].reshape(M * S, CF))
-                .astype(BF16)
-                .reshape(nz, 2, RF, CF)
-            )
+            if second:
+                grads = GC[...].reshape(M * S, D)
+                DWO[k, xx] = tn(AS[:, :, cols].reshape(M * S, CF), grads).astype(BF16)
+            if first:
+                part = tn(XB[...].reshape(M * S, D), GHS[:, :, cols].reshape(M * S, CF))
+                DWI[k, :, :, :, cols] = part.astype(BF16).reshape(nz, 2, RF, CF)
             return carry
 
         lax.fori_loop(0, 2, half, 0)
@@ -856,6 +855,42 @@
             )
             GCS[m, p, 0:1] = jnp.sum(jnp.where(diagonal, weight, 0.0), axis=0, keepdims=True)
         exchange(GCS, GCB, m, s_gc[m])
+
+    r_fin, s_fin = (sems.take(nz), sems.take(1)), (sends.take(1), sends.take(1))
+    FX = (b["FXI"], b["FXO"])
+    GI, GT = b["GI"], b["GT"]
+    sent_later(s_fin[0], FX[0])
+    sent_later(s_fin[1], FX[1])
+
+    def total_of(kind, place):
+        return (
+            OWN[kind][place].astype(F32)
+            + UP[kind][place].astype(F32)
+            + DN[kind][place].astype(F32)
+        )
+
+    def sums_end_in(k):
+        cols = pl.ds(pl.multiple_of(k * FC, 128), FC)
+        for side, ref, ok in ((0, UP, z > 0), (1, DN, z < nz - 1)):
+            arrived(ref[0].at[k, z], r_up[side][0] + k * nz + z, ok)
+        FX[0][k] = total_of(0, (k, z, 1 - x)).astype(BF16)
+        send(FX[0].at[k], GI.at[x, :, cols], s_fin[0], r_fin[0] + k, across)
+        GI[x, :, cols] = total_of(0, (k, z, x)).astype(BF16)
+
+    def sums_end_out(mine):
+        xx = x if mine else 1 - x
+        for side, ref, ok in ((0, UP, z > 0), (1, DN, z < nz - 1)):
+            arrived(ref[1].at[z, xx], r_up[side][1] + 2 * z + xx, ok)
+        if mine:
+            GT[x] = total_of(1, (z, xx)).astype(BF16)
+        else:
+            FX[1][...] = total_of(1, (z, xx)).astype(BF16)
+            send(FX[1], GT.at[x], s_fin[1], r_fin[1], across)
+
+    at_end = (z == 0) | (z == nz - 1)
+    upper = z // h
+    first_ends = [nz - 1 - upper * (nz - 1), 1 + upper * (nz - 3)]
+    last_ends = [upper * (nz - 1), 2 - upper * (5 - nz)] if nz == 4 else []
 
     when_two, when_far, when_late = (1, 2, nz - 1) if nz <= 4 else (0, 0, 0)
     for i in range(nz):
@@ -887,44 +922,10 @@
         if i == nz - 1:
             for m in range(M):
                 exchange(YS, YB, m, s_y[m])
-        expert_weights(block)
+        expert_weights(block, True, i > 0)
         sums_begin(i, (0, 1, 2) if i < nz - 1 else (0, 1, 3))
-
-    r_fin, s_fin = (sems.take(nz), sems.take(1)), (sends.take(1), sends.take(1))
-    FX = (b["FXI"], b["FXO"])
-    GI, GT = b["GI"], b["GT"]
-    sent_later(s_fin[0], FX[0])
-    sent_later(s_fin[1], FX[1])
-
-    def total_of(kind, place):
-        return (
-            OWN[kind][place].astype(F32)
-            + UP[kind][place].astype(F32)
-            + DN[kind][place].astype(F32)
-        )
-
-    def sums_end_in(k):
-        cols = pl.ds(pl.multiple_of(k * FC, 128), FC)
-        for side, ref, ok in ((0, UP, z > 0), (1, DN, z < nz - 1)):
-            arrived(ref[0].at[k, z], r_up[side][0] + k * nz + z, ok)
-        FX[0][k] = total_of(0, (k, z, 1 - x)).astype(BF16)
-        send(FX[0].at[k], GI.at[x, :, cols], s_fin[0], r_fin[0] + k, across)
-        GI[x, :, cols] = total_of(0, (k, z, x)).astype(BF16)
-
-    def sums_end_out(mine):
-        xx = x if mine else 1 - x
-        for side, ref, ok in ((0, UP, z > 0), (1, DN, z < nz - 1)):
-            arrived(ref[1].at[z, xx], r_up[side][1] + 2 * z + xx, ok)
-        if mine:
-            GT[x] = total_of(1, (z, xx)).astype(BF16)
-        else:
-            FX[1][...] = total_of(1, (z, xx)).astype(BF16)
-            send(FX[1], GT.at[x], s_fin[1], r_fin[1], across)
-
-    at_end = (z == 0) | (z == nz - 1)
-    upper = z // h
-    first_ends = [nz - 1 - upper * (nz - 1), 1 + upper * (nz - 3)]
-    last_ends = [upper * (nz - 1), 2 - upper * (5 - nz)] if nz == 4 else []
+        if i == 0:
+            expert_weights(block, False, True)
 
     def sums_close():
         kept.append(fetch(GI.at[x], gein.at[x]))
@@ -1067,7 +1068,7 @@
     arrived(SB3.at[1 - x], r_b3)
     SB4[z] = SB3[0] + SB3[1]
     s_b4, r_b4 = sends.take(1), sems.take(1)
-    for dz in orders:
+    for dz in far_first:
         send(SB4.at[z], SB4.at[z], s_b4, r_b4, at((z + dz) % nz, x, e))
     sent_later(s_b4, SB4.at[0 : nz - 1])
     sums_begin(nz - 1, (4,))

time: 135 us -> 134 us (level)
  no operation moved by 1% of the time
where the time goes in v2:
time: 134 us
  Pallas kernels  133 us (99%)
    pallas_call x1, Pallas kernels, body(): pl.pallas_call(functools.partial(kernel, c, names, counts), out_shape=hal...  130 us
    pallas_call x1, Pallas kernels, body(): pl.pallas_call(hand_over, out_shape=shapes, in_specs=[anywhere] * 9, out_...  3.15 us

profile of v2, /device:TPU:0, one launch (start us, length us, event | category | flops | bytes accessed | tf_op | source)
XLA Modules:
  0.0 133.8 jit_solution(11692491403472041145)
XLA Ops:
  0.6 129.8 %shard_map.169 = (bf16[197,2,512]{2,1,0:T(2,128)(2,1)}, f32[2,197,1,512]{3,2,1,0:T(1,128)}, bf16[64,1536]{1,0:T(8,128)(2,1)}, bf16[64,512]{1,0:T(8,128)(2,1)}, f...) custom-call(bf16[197,2,512]{2,1,0:T(2,128)(2,1)} %bitcast.21, ...), custom_call_target="tpu_custom_call" | custom-call | tf_op jit(solution)/shard_map/pallas_call | solution.py:1192
  130.5 3.2 %shard_map.170 = (bf16[197,2,512]{2,1,0:T(2,128)(2,1)}, f32[2,197,1,512]{3,2,1,0:T(1,128)}, f32[64,1536]{1,0:T(8,128)}, f32[64,512]{1,0:T(8,128)}, f32[1,64]{1,0...) custom-call(bf16[197,2,512]{2,1,0:T(2,128)(2,1)} %get-tuple-element.27.refs_0_, ...), custom_call_target="tpu_custom_call" | custom-call | tf_op jit(solution)/shard_map/pallas_call | solution.py:1214

commit v3 on v2

--- a/solution.py
+++ b/solution.py
@@ -85,11 +85,11 @@
     v = {
         "XP": ((M, TP, D), BF16),
         "CT": ((M, TP, D), BF16),
-        "XR": ((T, M, D), BF16),
-        "CR": ((T, M, D), BF16),
-        "AR": ((T, M, D), F32),
-        "AO": ((T, M, D), BF16),
-        "IG": ((M, T, 1, D), F32),
+        "XR": ((TP, M, D), BF16),
+        "CR": ((TP, M, D), BF16),
+        "AR": ((TP, M, D), F32),
+        "AO": ((TP, M, D), BF16),
+        "IG": ((M, TP, 1, D), F32),
         "RR": ((M, 2, T), jnp.int32),
         "RT": ((M, TP, 128), F32),
         "SR": ((nz, 2, NR, RF), BF16),
@@ -418,7 +418,7 @@
         fetch(gain2, b["G2"]),
         fetch(router, b["RW"]),
     ]
-    token_in = [fetch(routes, b["RR"]), fetch(xin, b["XR"]), fetch(cot, b["CR"])]
+    token_in = [fetch(routes, b["RR"]), fetch(xin, b["XR"].at[0:T]), fetch(cot, b["CR"].at[0:T])]
     own_in = locals_.take(1)
     for k in range(nz):
         pltpu.make_async_copy(
@@ -473,12 +473,12 @@
     swap = (
         lax.broadcasted_iota(jnp.int32, (2, 128), 0) == lax.broadcasted_iota(jnp.int32, (2, 128), 1)
     ).astype(BF16)
+    for ref in (b["XR"], b["CR"]):
+        ref[T:TP] = jnp.zeros((TP - T, M, D), BF16)
     for m in range(M):
-        XP[m] = jnp.zeros((TP, D), BF16)
-        CT[m] = jnp.zeros((TP, D), BF16)
         RT[m] = jnp.full((TP, 128), -1.0, F32)
-        XP[m, 0:T] = b["XR"][:, m, :]
-        CT[m, 0:T] = b["CR"][:, m, :]
+        XP[m] = b["XR"][:, m, :]
+        CT[m] = b["CR"][:, m, :]
         RT[m, 0:T] = tn(b["RR"][m].astype(BF16), swap)
 
     def onehot(m, j):
@@ -942,7 +942,7 @@
     def outputs(m):
         results = YB[m].reshape(S, D)
         out = MID[m] + chosen_of(m, 0) * nn(PM[m, 0], results)
-        b["AR"][:, m, :] = (out + chosen_of(m, 1) * nn(PM[m, 1], results))[0:T]
+        b["AR"][:, m, :] = out + chosen_of(m, 1) * nn(PM[m, 1], results)
 
     def backward_top(m):
         upstream = CT[m].astype(F32)
@@ -1008,7 +1008,7 @@
         hat, rstd = normalize(XP[m].astype(F32))
         GR[NE : NE + 1] = GR[NE : NE + 1] + jnp.sum(grad * hat, axis=0, keepdims=True)
         full = GM[m] + normalize_back(grad * gain_one, hat, rstd)
-        b["IG"][m, :, 0, :] = full[0:T]
+        b["IG"][m, :, 0, :] = full
         return carry
 
     if nz <= 4:
@@ -1033,7 +1033,7 @@
     GB, SB1, SB2, SB3, SB4 = (b[k] for k in ("GB", "SB1", "SB2", "SB3", "SB4"))
     qkv.sum_core()
     lax.fori_loop(0, M, backward_end, 0)
-    kept.append(fetch(b["IG"], igrad))
+    kept.append(fetch(b["IG"].at[:, 0:T], igrad))
     GB[...] = GR[...].astype(BF16)
     r_b1 = one_send(GB, SB1, sibling)
     qkv.sum_plane()
@@ -1104,7 +1104,7 @@
         exchanged(YB, m, s_y[m])
         outputs(m)
     b["AO"][...] = b["AR"][...].astype(BF16)
-    kept.append(fetch(b["AO"], act))
+    kept.append(fetch(b["AO"].at[0:T], act))
     arrived(SB4.at[0 : nz - 1], r_b4)
     total = SB4[0].astype(F32)
     for k in range(1, nz):

time: 134 us -> 134 us (level)
  no operation moved by 1% of the time
where the time goes in v3:
time: 134 us
  Pallas kernels  133 us (99%)
    pallas_call x1, Pallas kernels, body(): pl.pallas_call(functools.partial(kernel, c, names, counts), out_shape=hal...  130 us
    pallas_call x1, Pallas kernels, body(): pl.pallas_call(hand_over, out_shape=shapes, in_specs=[anywhere] * 9, out_...  3.15 us

profile of v3, /device:TPU:0, one launch (start us, length us, event | category | flops | bytes accessed | tf_op | source)
XLA Modules:
  0.0 133.7 jit_solution(3039350294696752818)
XLA Ops:
  0.6 129.8 %shard_map.169 = (bf16[197,2,512]{2,1,0:T(2,128)(2,1)}, f32[2,197,1,512]{3,2,1,0:T(1,128)}, bf16[64,1536]{1,0:T(8,128)(2,1)}, bf16[64,512]{1,0:T(8,128)(2,1)}, f...) custom-call(bf16[197,2,512]{2,1,0:T(2,128)(2,1)} %bitcast.21, ...), custom_call_target="tpu_custom_call" | custom-call | tf_op jit(solution)/shard_map/pallas_call | solution.py:1192
  130.4 3.2 %shard_map.170 = (bf16[197,2,512]{2,1,0:T(2,128)(2,1)}, f32[2,197,1,512]{3,2,1,0:T(1,128)}, f32[64,1536]{1,0:T(8,128)}, f32[64,512]{1,0:T(8,128)}, f32[1,64]{1,0...) custom-call(bf16[197,2,512]{2,1,0:T(2,128)(2,1)} %get-tuple-element.27.refs_0_, ...), custom_call_target="tpu_custom_call" | custom-call | tf_op jit(solution)/shard_map/pallas_call | solution.py:1214
